TPU v7x, 32 devices: a whole 2x2x4 slice. The times are simulated.
32 devices in a mesh: slot: 4 (over y, x), tile: 8 (over z, core).
Axes of the slice: x: 2, y: 2, z: 4, core: 2. Of those that a mesh axis runs over, the one named last changes fastest.
Arguments:
- control: float32 [1024], replicated, may hold values from -6 to 6
- anomalies: bfloat16 [4, 64, 262144], P('slot', None, 'tile'), may hold values from -0.75 to 0.75
- modes: bfloat16 [16, 262144], P(None, 'tile'), may hold values from -1.5 to 1.5
- interp: bfloat16 [4, 1024, 128, 128], P('slot', 'tile'), may hold values from -0.5 to 0.5
- block_index: int32 [4, 1024], P('slot', 'tile'), may hold values from 0 to 2047
- counts: int32 [4, 8], P('slot', 'tile'), may hold values from 64 to 128, as said below
- innovation: float32 [4, 1024, 128], P('slot', 'tile'), may hold values from -6 to 6
- obs_weight: float32 [4, 1024, 128], P('slot', 'tile'), may hold values from 0.005 to 0.05
Outputs:
- departure: float32 [4, 1024, 128], P('slot', 'tile')
- gradient: float32 [1024], P('tile')
Inputs may be any that keep to these rules, and one draw needn't show every extreme that they name: Only the first counts[g, j] of the 128 block slots of a device are observations; the others are ignored. Some device has all 128 live in every draw.
All inputs are finite; a program needn't handle non-finite values.
Results may differ from a plain program's by a relative error of at most 0.0027.
Values may be sent and summed in bfloat16 or wider, within the bound.
A program may use at most 64 MiB of HBM per device.

v0:
```python
import jax
import jax.numpy as jnp
from jax import lax
from jax.sharding import PartitionSpec as P

BLK = 128
HB = 128


def padded(cells, sides, width):
    for axis, dim in sides:
        count = lax.axis_size(axis)
        head = lax.slice_in_dim(cells, 0, width, axis=dim)
        tail = lax.slice_in_dim(cells, cells.shape[dim] - width, cells.shape[dim], axis=dim)
        cells = jnp.concatenate(
            [
                lax.ppermute(tail, axis, [(i, (i + 1) % count) for i in range(count)]),
                cells,
                lax.ppermute(head, axis, [((i + 1) % count, i) for i in range(count)]),
            ],
            axis=dim,
        )
    return cells


def from_behind(value, axis, steps):
    count = lax.axis_size(axis)
    pairs = [(source, (source + steps) % count) for source in range(count)]
    return lax.ppermute(value, axis, pairs)


def on_device(control, anomalies, modes, interp, block_index, counts, innovation, obs_weight):
    members = anomalies.shape[1]
    state_rows = anomalies.shape[2]
    width_modes = modes.shape[0]
    obs_blocks = interp.shape[1]
    rim_rows = HB * BLK
    batch_blocks = 16
    coarse = control.astype(jnp.bfloat16).reshape(members, width_modes)
    weights_rows = jnp.dot(coarse, modes, preferred_element_type=jnp.float32)
    increment = jnp.sum(anomalies[0] * weights_rows, axis=0)
    own_rows = increment.astype(jnp.bfloat16)[None, :]
    gathered = lax.all_gather(own_rows, "slot", axis=0, tiled=True)
    window = padded(gathered, (("tile", 1),), rim_rows)
    slot_count = window.shape[0]
    block_table = window.reshape(-1, BLK)
    live_count = counts[0, 0]
    group_turns = (live_count + batch_blocks - 1) // batch_blocks

    def visit_group(group_turn, state_pair):
        departed, window_sums = state_pair
        first_block = group_turn * batch_blocks
        block_mats = lax.dynamic_slice_in_dim(interp[0], first_block, batch_blocks, 0)
        block_picks = lax.dynamic_slice_in_dim(block_index[0], first_block, batch_blocks, 0)
        targets = lax.dynamic_slice_in_dim(innovation[0], first_block, batch_blocks, 0)
        scales = lax.dynamic_slice_in_dim(obs_weight[0], first_block, batch_blocks, 0)
        block_states = jnp.take(block_table, block_picks, axis=0)
        mapped = jnp.einsum(
            "bij,bj->bi", block_mats, block_states, preferred_element_type=jnp.float32
        )
        live_mask = first_block + jnp.arange(batch_blocks, dtype=jnp.int32) < live_count
        misfit = jnp.where(live_mask[:, None], mapped - targets, jnp.zeros_like(mapped))
        weighted = (scales * misfit).astype(jnp.bfloat16)
        pulled = jnp.einsum("bij,bi->bj", block_mats, weighted, preferred_element_type=jnp.float32)
        window_sums = window_sums.at[block_picks].add(pulled)
        departed = lax.dynamic_update_slice_in_dim(departed, misfit, first_block, 0)
        return (departed, window_sums)

    start_pair = (
        jnp.zeros((obs_blocks, BLK), jnp.float32),
        jnp.zeros(block_table.shape, jnp.float32),
    )
    departed, window_sums = lax.fori_loop(0, group_turns, visit_group, start_pair)
    adjoint_window = window_sums.reshape(slot_count, -1)
    from_above = from_behind(adjoint_window[:, :rim_rows].astype(jnp.bfloat16), "tile", -1).astype(
        jnp.float32
    )
    from_below = from_behind(
        adjoint_window[:, rim_rows + state_rows :].astype(jnp.bfloat16), "tile", 1
    ).astype(jnp.float32)
    own_sums = adjoint_window[:, rim_rows : rim_rows + state_rows]
    own_sums = (
        own_sums.at[:, state_rows - rim_rows :].add(from_above).at[:, :rim_rows].add(from_below)
    )
    adjoint_own = lax.psum_scatter(
        own_sums.astype(jnp.bfloat16), "slot", scatter_dimension=0, tiled=True
    ).astype(jnp.float32)[0]
    scaled = (adjoint_own[None, :] * modes).astype(jnp.bfloat16)
    partial_value = lax.dot_general(
        anomalies[0], scaled, (((1,), (1,)), ((), ())), preferred_element_type=jnp.float32
    )
    flat_partial = partial_value.reshape(-1)
    tile_count = lax.axis_size("tile")
    total_columns = members * width_modes
    share_size = total_columns // tile_count
    slot_summed = lax.psum(flat_partial, "slot")
    owned_share = lax.psum_scatter(slot_summed, "tile", scatter_dimension=0, tiled=True)
    share_start = lax.axis_index("tile") * share_size
    gradient = lax.dynamic_slice_in_dim(control, share_start, share_size, 0) + owned_share
    return (departed[None], gradient)


def solution(mesh):
    in_specs = (
        P(),
        P("slot", None, "tile"),
        P(None, "tile"),
        P("slot", "tile", None, None),
        P("slot", "tile"),
        P("slot", "tile"),
        P("slot", "tile", None),
        P("slot", "tile", None),
    )
    out_specs = (P("slot", "tile", None), P("tile"))
    return jax.shard_map(
        on_device, mesh=mesh, in_specs=in_specs, out_specs=out_specs, check_vma=False
    )
```

profile of v0, /device:TPU:0, one launch (start us, length us, event | category | flops | bytes accessed | tf_op | source)
XLA Modules:
  0.0 167.1 jit_solution(43339250250352734)
XLA Ops:
  8.0 3.8 %fusion.16 = bf16[32768]{0:T(1024)(128)(2,1)S(1)} fusion(bf16[64,16]{1,0:T(8,128)(2,1)S(1)} %reshape.116, bf16[16,32768]{1,0:T(8,128)(2,1)} %param.16, bf16[1,64,32768]{2,1,0:T(8,128)(2,1)} %param.15), kind=kOutput, calls=%fused_computation.29 | convolution fusion | flops 73367552 | bytes 5310464 | tf_op jit(solution)/shard_map/dot_general | solution.py:40
  11.8 10.4 %all-gather = bf16[131072]{0:T(1024)(128)(2,1)S(1)} all-gather(bf16[32768]{0:T(1024)(128)(2,1)S(1)} %fusion.16), channel_id=2, replica_groups=mesh['slot'=4,'tile'=8] {'slot'}, dimensions={0}, use_global_device_ids=true | all-gather | bytes 327680 | tf_op jit(solution)/shard_map/all_gather | solution.py:43
  22.5 3.5 %collective-permute-start.1 = (bf16[4,16384]{1,0:T(4,128)(2,1)S(1)}, bf16[4,16384]{1,0:T(4,128)(2,1)S(1)}, u32[]{:S(2)}, u32[]{:S(2)}) collective-permute-start(bf16[4,16384]{1,0:T(4,128)(2,1)S(1)} %get-tuple-element.109), channel_id=1, source_target_pairs={{1,0},{2,1},{3,2},{4,3},{5,4},{6,5},{7,6},{0,7},{9,8},{10,9},{11,1... | collective-permute-start | bytes 393224 | tf_op jit(solution)/shard_map/ppermute | solution.py:19
  26.7 2.1 %collective-permute-done = bf16[4,16384]{1,0:T(4,128)(2,1)S(1)} collective-permute-done((bf16[4,16384]{1,0:T(4,128)(2,1)S(1)}, bf16[4,16384]{1,0:T(4,128)(2,1)S(1)}, u32[]{:S(2)}, u32[]{:S(2)}) %collective-permute-start) | collective-permute-done | bytes 131104 | tf_op jit(solution)/shard_map/ppermute | solution.py:17
  29.6 30.2 %while.14 = (s32[]{:T(128)}, f32[128,128]{1,0:T(8,128)S(1)}, f32[2048,128]{1,0:T(8,128)S(1)}, s32[]{:T(128)}, s32[]{:T(128)}, /*index=5*/bf16[1,128,128,128]{3,2...) while((s32[]{:T(128)}, f32[128,128]{1,0:T(8,128)S(1)}, ...), condition=%wide.region_3.4_spmd, body=%wide.region_1.3_spmd.sunk | while | flops 1062070 | bytes 1156223 | solution.py:73
  31.1 1.4 fusion.40
  33.3 1.3 fusion.42
  34.6 1.1 scatter_fusion
  37.2 1.4 fusion.40
  38.6 0.8 fusion.41
  39.4 1.3 fusion.42
  40.7 1.1 scatter_fusion
  43.2 1.4 fusion.40
  44.6 0.8 fusion.41
  45.4 1.3 fusion.42
  46.7 1.1 scatter_fusion
  49.3 1.4 fusion.40
  50.7 0.8 fusion.41
  51.5 1.3 fusion.42
  52.8 1.1 scatter_fusion
  55.3 1.4 fusion.40
  56.7 0.8 fusion.41
  57.5 1.3 fusion.42
  58.8 1.1 scatter_fusion
  62.0 2.2 %collective-permute-done.2 = bf16[4,16384]{1,0:T(4,128)(2,1)S(1)} collective-permute-done((bf16[4,16384]{1,0:T(4,128)(2,1)S(1)}, bf16[4,16384]{1,0:T(4,128)(2,1)S(1)}, u32[]{:S(2)}, u32[]{:S(2)}) %collective-permute-start.2) | collective-permute-done | bytes 131104 | tf_op jit(solution)/shard_map/ppermute | solution.py:29
  64.2 3.4 %collective-permute-done.3 = bf16[4,16384]{1,0:T(4,128)(2,1)S(1)} collective-permute-done((bf16[4,16384]{1,0:T(4,128)(2,1)S(1)}, bf16[4,16384]{1,0:T(4,128)(2,1)S(1)}, u32[]{:S(2)}, u32[]{:S(2)}) %collective-permute-start.3) | collective-permute-done | bytes 131104 | tf_op jit(solution)/shard_map/ppermute | solution.py:29
  71.2 57.6 %all-reduce.4.cloned.1.call-done = bf16[4,32768]{1,0:T(4,128)(2,1)} async-done(((bf16[4,32768]{1,0:T(4,128)(2,1)}), bf16[4,32768]{1,0:T(4,128)(2,1)}) %all-reduce.4.cloned.1.call-update) | async-done | bytes 262160
  128.8 1.7 %dynamic-slice_convert_fusion = f32[1,32768]{1,0:T(1,128)S(1)} fusion(bf16[4,32768]{1,0:T(4,128)(2,1)} %all-reduce.4.cloned.1.call-done, u32[]{:T(128)} %bitcast.17), kind=kLoop, calls=%fused_computation.38 | loop fusion | flops 32768 | bytes 196612 | tf_op jit(solution)/shard_map/mul | solution.py:88
  130.6 3.4 %fusion.17 = f32[64,16]{0,1:T(8,128)S(1)} fusion(bf16[1,64,32768]{2,1,0:T(8,128)(2,1)} %param.15, bf16[16,32768]{1,0:T(8,128)(2,1)S(1)} %copy-done, f32[32768]{0:T(1024)S(1)} %bitcast.75), kind=kOutput, calls=%fused_computation.31 | convolution fusion | flops 68681728 | bytes 5378048 | tf_op jit(solution)/shard_map/dot_general | solution.py:89
  134.1 15.9 %all-reduce.1 = f32[1024]{0:T(1024)S(1)} all-reduce(f32[1024]{0:T(1024)S(1)} %reshape.119), channel_id=4, replica_groups=mesh['slot'=4,'tile'=8] {'tile'}, use_global_device_ids=true, to_apply=%region_7.8.clone | all-reduce | flops 1024 | bytes 8192
  150.1 8.9 %psum.8 = f32[128]{0:T(128)S(1)} all-reduce(f32[128]{0:T(128)S(1)} %dynamic-slice.23), channel_id=1, replica_groups=mesh['slot'=4,'tile'=8] {'slot'}, use_global_device_ids=true, to_apply=%region_6.7 | all-reduce | flops 128 | bytes 1024 | tf_op jit(solution)/shard_map/psum | solution.py:96
  159.0 1.3 dynamic-slice_add_fusion
  (63 shorter events, 15.2 us)
Async XLA Ops:
  7.2 121.7 %all-reduce.4.cloned.1.call-start = ((), (), s32[]{:S(2)}) async-start(), calls=%async_computation | async-start | bytes 524288
  8.0 21.6 %copy-start.2 = (s32[1,128]{1,0:T(1,128)S(1)}, s32[1,128]{1,0:T(1,128)}, u32[]{:S(2)}) copy-start(s32[1,128]{1,0:T(1,128)} %param.18) | copy-start | bytes 1540
  22.4 6.3 %collective-permute-start = (bf16[4,16384]{1,0:T(4,128)(2,1)S(1)}, bf16[4,16384]{1,0:T(4,128)(2,1)S(1)}, u32[]{:S(2)}, u32[]{:S(2)}) collective-permute-start(bf16[4,16384]{1,0:T(4,128)(2,1)S(1)} %get-tuple-element.108), channel_id=1, source_target_pairs={{0,1},{1,2},{2,3},{3,4},{4,5},{5,6},{6,7},{7,0},{8,9},{9,10},{10,1... | collective-permute-start | bytes 393224 | tf_op jit(solution)/shard_map/ppermute | solution.py:17
  22.5 6.3 %collective-permute-start.1 = (bf16[4,16384]{1,0:T(4,128)(2,1)S(1)}, bf16[4,16384]{1,0:T(4,128)(2,1)S(1)}, u32[]{:S(2)}, u32[]{:S(2)}) collective-permute-start(bf16[4,16384]{1,0:T(4,128)(2,1)S(1)} %get-tuple-element.109), channel_id=1, source_target_pairs={{1,0},{2,1},{3,2},{4,3},{5,4},{6,5},{7,6},{0,7},{9,8},{10,9},{11,1... | collective-permute-start | bytes 393224 | tf_op jit(solution)/shard_map/ppermute | solution.py:19
  59.9 74.0 %copy-start.1 = (f32[128,128]{1,0:T(8,128)}, f32[128,128]{1,0:T(8,128)S(1)}, u32[]{:S(2)}) copy-start(f32[128,128]{1,0:T(8,128)S(1)} %get-tuple-element.80) | copy-start | bytes 196612
  59.9 9.4 %copy-start.4 = (u32[32]{0:T(128)S(1)}, u32[32]{0:T(128)}, u32[]{:S(2)}) copy-start(u32[32]{0:T(128)} %constant.126) | copy-start | bytes 388
  59.9 9.9 %copy-start.3 = (u32[32]{0:T(128)S(1)}, u32[32]{0:T(128)}, u32[]{:S(2)}) copy-start(u32[32]{0:T(128)} %constant.130) | copy-start | bytes 388
  59.9 70.6 %copy-start = (bf16[16,32768]{1,0:T(8,128)(2,1)S(1)}, bf16[16,32768]{1,0:T(8,128)(2,1)}, u32[]{:S(2)}) copy-start(bf16[16,32768]{1,0:T(8,128)(2,1)} %param.16) | copy-start | bytes 3145732
  60.7 3.5 %collective-permute-start.2 = (bf16[4,16384]{1,0:T(4,128)(2,1)S(1)}, bf16[4,16384]{1,0:T(4,128)(2,1)S(1)}, u32[]{:S(2)}, u32[]{:S(2)}) collective-permute-start(bf16[4,16384]{1,0:T(4,128)(2,1)S(1)} %get-tuple-element.107), channel_id=1, source_target_pairs={{0,7},{1,0},{2,1},{3,2},{4,3},{5,4},{6,5},{7,6},{8,15},{9,8},{10,9... | collective-permute-start | bytes 393224 | tf_op jit(solution)/shard_map/ppermute | solution.py:29
  61.4 6.2 %collective-permute-start.3 = (bf16[4,16384]{1,0:T(4,128)(2,1)S(1)}, bf16[4,16384]{1,0:T(4,128)(2,1)S(1)}, u32[]{:S(2)}, u32[]{:S(2)}) collective-permute-start(bf16[4,16384]{1,0:T(4,128)(2,1)S(1)} %get-tuple-element.106), channel_id=1, source_target_pairs={{0,1},{1,2},{2,3},{3,4},{4,5},{5,6},{6,7},{7,0},{8,9},{9,10},{10,1... | collective-permute-start | bytes 393224 | tf_op jit(solution)/shard_map/ppermute | solution.py:29
Sparse Core Ops, SparseCore 0:
  69.4 59.4 all-reduce.3
where the time goes:
time: 168 us; the launch traced here: 167 us
  waiting for transfers between devices  65.3 us (39%)
  blocking collectives  35.3 us (21%)
  matrix products  20.5 us (12%)
  other arithmetic  20.2 us (12%)
  between operations  15.6 us (9%)
  local copies, waits for them, and re-layouts  5.86 us (3%)
  starting transfers between devices  4.23 us (3%)
    unnamed x2, waiting for transfers between devices  57.6 us
    unnamed x1, blocking collectives  15.9 us
    all_gather x1, blocking collectives, on_device(): gathered = lax.all_gather(own_rows, 'slot', axis=0, tiled=True)  10.4 us
    psum x1, blocking collectives, on_device(): slot_summed = lax.psum(flat_partial, 'slot')  8.89 us
    dot_general x5, matrix products, visit_group(): jnp.einsum('bij,bj->bi', block_mats, block_states, preferred_element_type...  6.98 us
    dot_general x5, matrix products, visit_group(): jnp.einsum('bij,bi->bj', block_mats, weighted, preferred_element_type=jnp...  6.39 us
    ppermute x2, waiting for transfers between devices, from_behind(): return lax.ppermute(value, axis, pairs)  5.6 us
    scatter-add x5, other arithmetic, visit_group(): window_sums = window_sums.at[block_picks].add(pulled)  5.31 us
  transfers between devices with their start and end apart: 5, of which 4 were waited for; matrix products, arithmetic and copies ran while one was open for 1% of the time, Pallas kernels for 0%

commit v1 on v0

v1 whole, which is shorter than its diff:
```python
import functools

import jax
import jax.numpy as jnp
from jax import lax
from jax.experimental import pallas as pl
from jax.experimental.pallas import tpu as pltpu
from jax.sharding import PartitionSpec as P

BLK = 128
HB = 128
STEP = 16
MESH = pl.DeviceIdType.MESH
NT = (((1,), (1,)), ((), ()))


def kernel(
    slots,
    tiles,
    ctl_ref,
    idx_ref,
    cnt_ref,
    anom_hbm,
    modes_hbm,
    interp_hbm,
    innov_hbm,
    wt_hbm,
    dep_hbm,
    grad_ref,
    anom,
    modes,
    interp,
    innov,
    wt,
    dep,
    coarse,
    idxs,
    pick_hot,
    add_hot,
    win,
    picks,
    got,
    states,
    pulled,
    edge_out,
    edge_in,
    adj,
    gs,
    gr,
    g2,
    local_sem,
    idx_sem,
    edge_sem,
    pick_sem,
    pull_sem,
    back_sem,
    g1_sem,
    g2_sem,
):
    s = lax.axis_index("slot")
    t = lax.axis_index("tile")
    members, rows = anom.shape
    width = modes.shape[0]
    blocks = rows // BLK
    obs = interp.shape[0]
    reach = blocks + 2 * HB
    parts = 4
    part_rows = rows // parts
    f32 = jnp.float32
    bf16 = jnp.bfloat16
    lower = lax.rem(t + tiles - 1, tiles)
    upper = lax.rem(t + 1, tiles)

    def slot_plus(d):
        return (lax.rem(s + d, slots), t)

    def slot_minus(d):
        return (lax.rem(s + slots - d, slots), t)

    def remote(src, dst, sems, i, target):
        return pltpu.make_async_remote_copy(
            src_ref=src,
            dst_ref=dst,
            send_sem=sems.at[0, i],
            recv_sem=sems.at[1, i],
            device_id=target,
            device_id_type=MESH,
        )

    loads = []
    for c in range(parts):
        cols = pl.ds(c * part_rows, part_rows)
        pair = (
            pltpu.make_async_copy(modes_hbm.at[:, cols], modes.at[:, cols], local_sem.at[2 * c]),
            pltpu.make_async_copy(anom_hbm.at[:, cols], anom.at[:, cols], local_sem.at[2 * c + 1]),
        )
        for copy in pair:
            copy.start()
        loads.append(pair)
    base = 2 * parts
    load_interp = pltpu.make_async_copy(interp_hbm, interp, local_sem.at[base])
    load_innov = pltpu.make_async_copy(innov_hbm, innov, local_sem.at[base + 1])
    load_wt = pltpu.make_async_copy(wt_hbm, wt, local_sem.at[base + 2])
    load_interp.start()
    load_innov.start()
    load_wt.start()

    barrier = pltpu.get_barrier_semaphore()
    for d in range(1, slots):
        pl.semaphore_signal(barrier, inc=1, device_id=slot_plus(d), device_id_type=MESH)
    for e in range(1, tiles):
        pl.semaphore_signal(
            barrier, inc=1, device_id=(s, lax.rem(t + e, tiles)), device_id_type=MESH
        )

    idxs[0] = jnp.broadcast_to(idx_ref[...], (8, BLK))

    per_row = BLK // width
    ctl = ctl_ref[...].astype(bf16)
    crows = ctl.shape[0]
    spread = (
        lax.broadcasted_iota(jnp.int32, (members, crows), 0) // per_row
        == lax.broadcasted_iota(jnp.int32, (members, crows), 1)
    )
    spread = jnp.where(spread, 1.0, 0.0).astype(bf16)
    wide = jnp.dot(spread, ctl, preferred_element_type=f32)
    lane = lax.broadcasted_iota(jnp.int32, (members, BLK), 1)
    member = lax.broadcasted_iota(jnp.int32, (members, BLK), 0)
    wide = jnp.where(lane // width == lax.rem(member, per_row), wide, 0.0).astype(bf16)
    fold = (
        lax.rem(lax.broadcasted_iota(jnp.int32, (width, BLK), 1), width)
        == lax.broadcasted_iota(jnp.int32, (width, BLK), 0)
    )
    fold = jnp.where(fold, 1.0, 0.0).astype(bf16)
    coarse[...] = lax.dot_general(fold, wide, NT, preferred_element_type=f32).astype(bf16)

    pl.semaphore_wait(barrier, slots - 1 + tiles - 1)

    idx_copies = []
    for d in range(1, slots):
        copy = remote(idxs.at[0], idxs.at[d], idx_sem, d, slot_plus(d))
        copy.start()
        idx_copies.append(copy)

    def increments(c):
        def body(i, carry):
            cols = pl.ds(pl.multiple_of(c * part_rows + i * (STEP * BLK), STEP * BLK), STEP * BLK)
            mixed = jnp.dot(coarse[...], anom[:, cols], preferred_element_type=f32)
            prod = mixed * modes[:, cols].astype(f32)
            sums = jnp.concatenate(
                [
                    jnp.sum(prod[:, j * BLK : (j + 1) * BLK], axis=0, keepdims=True)
                    for j in range(STEP)
                ],
                axis=0,
            )
            first = pl.multiple_of(HB + c * (part_rows // BLK) + i * STEP, STEP)
            win[pl.ds(first, STEP), :] = sums.astype(bf16)
            return carry

        lax.fori_loop(0, part_rows // (STEP * BLK), body, 0)

    for c in range(parts // 2):
        for copy in loads[c]:
            copy.wait()
        increments(c)
    to_lower = remote(
        win.at[pl.ds(HB, HB)], win.at[pl.ds(HB + blocks, HB)], edge_sem, 0, (s, lower)
    )
    to_lower.start()
    for c in range(parts // 2, parts):
        for copy in loads[c]:
            copy.wait()
        increments(c)
    to_upper = remote(win.at[pl.ds(blocks, HB)], win.at[pl.ds(0, HB)], edge_sem, 1, (s, upper))
    to_upper.start()

    origin = s * reach
    for d in range(slots):
        if d > 0:
            idx_copies[d - 1].wait_recv()
        row = idxs[d, 0:1, :]
        shifted = jnp.broadcast_to((row - origin).astype(f32), (obs, BLK))
        column = jnp.transpose(shifted)
        for q in range(reach // BLK):
            at = (lax.broadcasted_iota(jnp.int32, (obs, BLK), 1) + q * BLK).astype(f32)
            pick_hot[d, :, q * BLK : (q + 1) * BLK] = jnp.where(column == at, 1.0, 0.0).astype(bf16)
            at = (lax.broadcasted_iota(jnp.int32, (BLK, obs), 0) + q * BLK).astype(f32)
            add_hot[q * BLK : (q + 1) * BLK, d * obs : (d + 1) * obs] = jnp.where(
                shifted == at, 1.0, 0.0
            ).astype(bf16)

    to_lower.wait_recv()
    to_upper.wait_recv()

    pick_copies = []
    for d in range(1, slots):
        picks[d] = jnp.dot(pick_hot[d], win[...], preferred_element_type=f32).astype(bf16)
        copy = remote(picks.at[d], got.at[d], pick_sem, d, slot_minus(d))
        copy.start()
        pick_copies.append(copy)
    total = jnp.dot(pick_hot[0], win[...], preferred_element_type=f32)
    load_interp.wait()
    load_innov.wait()
    load_wt.wait()
    for d in range(1, slots):
        pick_copies[d - 1].wait_recv()
        total = total + got[d].astype(f32)
    states[...] = total.astype(bf16)

    live = cnt_ref[0, 0]
    sub = lax.broadcasted_iota(jnp.int32, (STEP, BLK), 0)

    def observe(g, carry):
        first = pl.multiple_of(g * STEP, STEP)
        mats = interp[pl.ds(first, STEP)].reshape(STEP * BLK, BLK)
        mapped_all = lax.dot_general(
            states[pl.ds(first, STEP), :], mats, NT, preferred_element_type=f32
        )
        mapped = mapped_all[:, 0:BLK]
        for r in range(1, STEP):
            mapped = jnp.where(sub == r, mapped_all[:, r * BLK : (r + 1) * BLK], mapped)
        misfit = jnp.where(
            sub + first < live, mapped - innov[pl.ds(first, STEP), :], jnp.zeros_like(mapped)
        )
        dep[pl.ds(first, STEP), :] = misfit
        weighted = wt[pl.ds(first, STEP), :] * misfit
        spread_w = jnp.concatenate(
            [jnp.where(sub == r, weighted, 0.0).astype(bf16) for r in range(STEP)], axis=1
        )
        pulled[pl.ds(first, STEP), :] = jnp.dot(
            spread_w, mats, preferred_element_type=f32
        ).astype(bf16)
        return carry

    lax.fori_loop(0, obs // STEP, observe, 0)

    pull_copies = []
    for d in range(1, slots):
        copy = remote(
            pulled.at[pl.ds(0, obs)], pulled.at[pl.ds(d * obs, obs)], pull_sem, d, slot_plus(d)
        )
        copy.start()
        pull_copies.append(copy)
    store_dep = pltpu.make_async_copy(dep, dep_hbm, local_sem.at[base + 3])
    store_dep.start()
    for copy in pull_copies:
        copy.wait_recv()

    edge_out[0] = jnp.dot(add_hot[0:HB, :], pulled[...], preferred_element_type=f32).astype(bf16)
    back_lower = remote(edge_out.at[0], edge_in.at[1], back_sem, 0, (s, lower))
    back_lower.start()
    edge_out[1] = jnp.dot(
        add_hot[HB + blocks : reach, :], pulled[...], preferred_element_type=f32
    ).astype(bf16)
    back_upper = remote(edge_out.at[1], edge_in.at[0], back_sem, 1, (s, upper))
    back_upper.start()
    adj[...] = jnp.dot(add_hot[HB : HB + blocks, :], pulled[...], preferred_element_type=f32)
    back_lower.wait_recv()
    back_upper.wait_recv()
    adj[0:HB, :] = adj[0:HB, :] + edge_in[0].astype(f32)
    adj[blocks - HB : blocks, :] = adj[blocks - HB : blocks, :] + edge_in[1].astype(f32)

    def project(i, acc):
        cols = pl.ds(pl.multiple_of(i * (STEP * BLK), STEP * BLK), STEP * BLK)
        rows_adj = adj[pl.ds(pl.multiple_of(i * STEP, STEP), STEP), :]
        part = modes[:, cols].astype(f32)
        scaled = jnp.concatenate(
            [
                (part[:, j * BLK : (j + 1) * BLK] * rows_adj[j : j + 1, :]).astype(bf16)
                for j in range(STEP)
            ],
            axis=1,
        )
        return acc + lax.dot_general(anom[:, cols], scaled, NT, preferred_element_type=f32)

    acc = lax.fori_loop(0, blocks // STEP, project, jnp.zeros((members, width), f32))

    share_rows = members // tiles
    wide = jnp.concatenate([acc] * per_row, axis=1)
    wide = jnp.where(lane // width == lax.rem(member, share_rows), wide, 0.0)
    for j in range(tiles):
        gs[j] = jnp.sum(wide[j * share_rows : (j + 1) * share_rows, :], axis=0, keepdims=True)

    g1_copies = []
    for e in range(1, tiles):
        to = lax.rem(t + e, tiles)
        copy = remote(gs.at[to], gr.at[e], g1_sem, e, (s, to))
        copy.start()
        g1_copies.append(copy)
    share = gs[t]
    for e in range(1, tiles):
        g1_copies[e - 1].wait_recv()
        share = share + gr[e]
    g2[0] = share
    g2_copies = []
    for d in range(1, slots):
        copy = remote(g2.at[0], g2.at[d], g2_sem, d, slot_plus(d))
        copy.start()
        g2_copies.append(copy)
    for d in range(1, slots):
        g2_copies[d - 1].wait_recv()
        share = share + g2[d]
    grad_ref[...] = share

    store_dep.wait()
    for copy in (
        idx_copies
        + [to_lower, to_upper]
        + pick_copies
        + pull_copies
        + [back_lower, back_upper]
        + g1_copies
        + g2_copies
    ):
        copy.wait_send()


def on_device(
    slots, tiles, control, anomalies, modes, interp, block_index, counts, innovation, obs_weight
):
    members, rows = anomalies.shape[1:]
    width = modes.shape[0]
    obs = interp.shape[1]
    blocks = rows // BLK
    reach = blocks + 2 * HB
    f32 = jnp.float32
    bf16 = jnp.bfloat16
    vmem = pl.BlockSpec(memory_space=pltpu.VMEM)
    hbm = pl.BlockSpec(memory_space=pl.ANY)

    def sems(n):
        return pltpu.SemaphoreType.DMA((2, n))

    departure, grad = pl.pallas_call(
        functools.partial(kernel, slots, tiles),
        out_shape=(
            jax.ShapeDtypeStruct((obs, BLK), f32),
            jax.ShapeDtypeStruct((1, BLK), f32),
        ),
        in_specs=[vmem, vmem, pl.BlockSpec(memory_space=pltpu.SMEM)] + [hbm] * 5,
        out_specs=(hbm, vmem),
        scratch_shapes=[
            pltpu.VMEM((members, rows), bf16),
            pltpu.VMEM((width, rows), bf16),
            pltpu.VMEM((obs, BLK, BLK), bf16),
            pltpu.VMEM((obs, BLK), f32),
            pltpu.VMEM((obs, BLK), f32),
            pltpu.VMEM((obs, BLK), f32),
            pltpu.VMEM((width, members), bf16),
            pltpu.VMEM((slots, 8, BLK), jnp.int32),
            pltpu.VMEM((slots, obs, reach), bf16),
            pltpu.VMEM((reach, slots * obs), bf16),
            pltpu.VMEM((reach, BLK), bf16),
            pltpu.VMEM((slots, obs, BLK), bf16),
            pltpu.VMEM((slots, obs, BLK), bf16),
            pltpu.VMEM((obs, BLK), bf16),
            pltpu.VMEM((slots * obs, BLK), bf16),
            pltpu.VMEM((2, HB, BLK), bf16),
            pltpu.VMEM((2, HB, BLK), bf16),
            pltpu.VMEM((blocks, BLK), f32),
            pltpu.VMEM((tiles, 1, BLK), f32),
            pltpu.VMEM((tiles, 1, BLK), f32),
            pltpu.VMEM((slots, 1, BLK), f32),
            pltpu.SemaphoreType.DMA((12,)),
            sems(slots),
            sems(2),
            sems(slots),
            sems(slots),
            sems(2),
            sems(tiles),
            sems(slots),
        ],
        compiler_params=pltpu.CompilerParams(
            collective_id=0, has_side_effects=True, vmem_limit_bytes=56 * 1024 * 1024
        ),
    )(
        control.reshape(-1, BLK),
        block_index,
        counts,
        anomalies[0],
        modes,
        interp[0],
        innovation[0],
        obs_weight[0],
    )
    share = control.shape[0] // tiles
    start = lax.axis_index("tile") * share
    gradient = lax.dynamic_slice_in_dim(control, start, share, 0) + grad[0, :share]
    return departure[None], gradient


def solution(mesh):
    in_specs = (
        P(),
        P("slot", None, "tile"),
        P(None, "tile"),
        P("slot", "tile", None, None),
        P("slot", "tile"),
        P("slot", "tile"),
        P("slot", "tile", None),
        P("slot", "tile", None),
    )
    out_specs = (P("slot", "tile", None), P("tile"))
    return jax.shard_map(
        functools.partial(on_device, mesh.shape["slot"], mesh.shape["tile"]),
        mesh=mesh,
        in_specs=in_specs,
        out_specs=out_specs,
        check_vma=False,
    )
```

time: 168 us -> 41 us (0.24)
  waiting for transfers between devices: 65.3 us -> 0 us
  Pallas kernels: 0 us -> 36.7 us
  blocking collectives: 35.3 us -> 0 us
  matrix products: 20.5 us -> 0 us
  other arithmetic: 20.2 us -> 1.28 us
  between operations: 15.6 us -> 1.29 us
  local copies, waits for them, and re-layouts: 5.86 us -> 1.47 us
  starting transfers between devices: 4.23 us -> 0 us
    unnamed x2 -> x0, waiting for transfers between devices: 57.6 us -> none
    pallas_call x0 -> x1, Pallas kernels: none -> 36.7 us  [on_device(): pl.pallas_call(functools.partial(kernel, slots, tiles), out_shape=(jax.Sh...]
    dot_general x12 -> x0, matrix products: 20.5 us -> none  [the longest x5 6.98 us: visit_group(): jnp.einsum('bij,bj->bi', block_mats, block_states, preferred_element_type...]
    unnamed x1 -> x0, blocking collectives: 15.9 us -> none
    all_gather x1 -> x0, blocking collectives: 10.4 us -> none  [on_device(): gathered = lax.all_gather(own_rows, 'slot', axis=0, tiled=True)]
    psum x1 -> x0, blocking collectives: 8.89 us -> none  [on_device(): slot_summed = lax.psum(flat_partial, 'slot')]
    ppermute x4 -> x0, waiting for transfers between devices: 7.68 us -> none  [the longest x2 5.6 us: from_behind(): return lax.ppermute(value, axis, pairs)]
    scatter-add x7 -> x0, other arithmetic: 6.16 us -> none  [the longest x5 5.31 us: visit_group(): window_sums = window_sums.at[block_picks].add(pulled)]
  transfers between devices with their start and end apart: 5 -> 0, of which waited for: 4 -> 0; matrix products, arithmetic and copies ran while one was open for 1% -> 0% of each run, Pallas kernels for 0% -> 0%
where the time goes in v1:
time: 41 us; the launch traced here: 40.8 us
  Pallas kernels  36.7 us (90%)
  local copies, waits for them, and re-layouts  1.47 us (4%)
  between operations  1.29 us (3%)
  other arithmetic  1.28 us (3%)
    pallas_call x1, Pallas kernels, on_device(): pl.pallas_call(functools.partial(kernel, slots, tiles), out_shape=(jax.Sh...  36.7 us
    unnamed x1, local copies, waits for them, and re-layouts  1.47 us
    add x1, other arithmetic, on_device(): lax.dynamic_slice_in_dim(control, start, share, 0) + grad[0, :share]  1.28 us

profile of v1, /device:TPU:0, one launch (start us, length us, event | category | flops | bytes accessed | tf_op | source)
XLA Modules:
  0.0 40.8 jit_solution(39531629045514612)
XLA Ops:
  1.3 36.7 %shard_map.95 = (f32[128,128]{1,0:T(8,128)}, f32[1,128]{1,0:T(1,128)}) custom-call(f32[8,128]{1,0:T(8,128)} %bitcast.13, s32[1,128]{1,0:T(1,128)} %idx_ref.1, s32[1,1]{1,0:T(1,128)S(6)} %copy.11.cnt_ref, bf16[64,32768]{1,0:T(8,128)(2,1)} %bitcast.8, bf16[16,32768]{1,0:T(8,128)(2,1)} %modes_hbm.1, bf16[128,128,128]{2,1,0:T(8,128)(2,1)} %bitcast.9, ...), custom_call_target="tpu_custom_call" | custom-call | tf_op jit(solution)/shard_map/pallas_call | solution.py:335
  38.0 1.3 %bitcast_add_fusion = f32[128]{0:T(128)} fusion(f32[1,128]{1,0:T(1,128)} %get-tuple-element.5, f32[1024]{0:T(1024)} %param.8, s32[]{:T(128)S(6)} %select_n.3), kind=kLoop, calls=%fused_computation | loop fusion | flops 128 | bytes 1540 | tf_op jit(solution)/shard_map/add | solution.py:389
  39.3 1.5 %copy.12 = f32[1,128,128]{2,1,0:T(8,128)} copy(f32[1,128,128]{2,1,0:T(8,128)} %bitcast.12) | data formatting | bytes 131072

commit v2 on v1

v2 whole, which is shorter than its diff:
```python
import functools

import jax
import jax.numpy as jnp
from jax import lax
from jax.experimental import pallas as pl
from jax.experimental.pallas import tpu as pltpu
from jax.sharding import PartitionSpec as P

BLK = 128
HB = 128
STEP = 16
MESH = pl.DeviceIdType.MESH
NT = (((1,), (1,)), ((), ()))


def kernel(
    slots,
    tiles,
    ctl_ref,
    idx_ref,
    cnt_ref,
    anom_hbm,
    modes_hbm,
    interp_hbm,
    innov_hbm,
    wt_hbm,
    dep_hbm,
    grad_ref,
    anom,
    modes,
    interp,
    innov,
    wt,
    dep,
    coarse,
    idxs,
    pick_hot,
    add_hot,
    edge_pick,
    edge_add,
    win,
    edges,
    picks,
    got,
    states,
    pulled,
    edge_out,
    edge_back,
    inner_out,
    inner_back,
    adj,
    gs,
    gp,
    gr,
    local_sem,
    idx_sem,
    edge_sem,
    core_sem,
    pick_sem,
    pull_sem,
    back_sem,
    g_sem,
):
    s = lax.axis_index("slot")
    t = lax.axis_index("tile")
    members, rows = anom.shape
    width = modes.shape[0]
    blocks = rows // BLK
    obs = interp.shape[0]
    reach = blocks + 2 * HB
    f32 = jnp.float32
    bf16 = jnp.bfloat16
    chips = tiles // 2
    z = t // 2
    core = lax.rem(t, 2)
    partner = (s, t + 1 - 2 * core)
    outer = lax.rem(t + tiles - 1 + 2 * core, tiles)
    halves = (core, 1 - core)

    def slot_plus(d, tile=None):
        return (lax.rem(s + d, slots), t if tile is None else tile)

    def slot_minus(d):
        return (lax.rem(s + slots - d, slots), t)

    def remote(src, dst, sems, i, target):
        return pltpu.make_async_remote_copy(
            src_ref=src,
            dst_ref=dst,
            send_sem=sems.at[0, i],
            recv_sem=sems.at[1, i],
            device_id=target,
            device_id_type=MESH,
        )

    parts = 4
    part_rows = rows // parts
    starts = [
        pl.multiple_of(half * (rows // 2) + q * part_rows, part_rows)
        for half in halves
        for q in range(2)
    ]
    loads = []
    for c in range(parts):
        cols = pl.ds(starts[c], part_rows)
        pair = (
            pltpu.make_async_copy(modes_hbm.at[:, cols], modes.at[:, cols], local_sem.at[2 * c]),
            pltpu.make_async_copy(anom_hbm.at[:, cols], anom.at[:, cols], local_sem.at[2 * c + 1]),
        )
        for copy in pair:
            copy.start()
        loads.append(pair)
    base = 2 * parts
    load_interp = pltpu.make_async_copy(interp_hbm, interp, local_sem.at[base])
    load_innov = pltpu.make_async_copy(innov_hbm, innov, local_sem.at[base + 1])
    load_wt = pltpu.make_async_copy(wt_hbm, wt, local_sem.at[base + 2])
    load_interp.start()
    load_innov.start()
    load_wt.start()

    barrier = pltpu.get_barrier_semaphore()
    pl.semaphore_signal(barrier, inc=1, device_id=partner, device_id_type=MESH)
    greeted = 1
    for d in range(slots):
        for e in range(chips):
            if d or e:
                to = (lax.rem(s + d, slots), lax.rem(z + e, chips) * 2 + core)
                pl.semaphore_signal(barrier, inc=1, device_id=to, device_id_type=MESH)
                greeted += 1
    for d in range(slots):
        pl.semaphore_signal(barrier, inc=1, device_id=slot_plus(d, outer), device_id_type=MESH)
        greeted += 1

    idxs[0] = jnp.broadcast_to(idx_ref[...], (8, BLK))

    per_row = BLK // width
    ctl = ctl_ref[...].astype(bf16)
    crows = ctl.shape[0]
    spread = (
        lax.broadcasted_iota(jnp.int32, (members, crows), 0) // per_row
        == lax.broadcasted_iota(jnp.int32, (members, crows), 1)
    )
    spread = jnp.where(spread, 1.0, 0.0).astype(bf16)
    wide = jnp.dot(spread, ctl, preferred_element_type=f32)
    lane = lax.broadcasted_iota(jnp.int32, (members, BLK), 1)
    member = lax.broadcasted_iota(jnp.int32, (members, BLK), 0)
    wide = jnp.where(lane // width == lax.rem(member, per_row), wide, 0.0).astype(bf16)
    fold = (
        lax.rem(lax.broadcasted_iota(jnp.int32, (width, BLK), 1), width)
        == lax.broadcasted_iota(jnp.int32, (width, BLK), 0)
    )
    fold = jnp.where(fold, 1.0, 0.0).astype(bf16)
    coarse[...] = lax.dot_general(fold, wide, NT, preferred_element_type=f32).astype(bf16)

    half_blocks = blocks // 2
    half_at = [pl.multiple_of(half * half_blocks, half_blocks) for half in halves]

    def increments(h, q):
        def body(i, carry):
            block = half_at[h] + q * (half_blocks // 2) + i * STEP
            block = pl.multiple_of(block, STEP)
            cols = pl.ds(pl.multiple_of(block * BLK, STEP * BLK), STEP * BLK)
            mixed = jnp.dot(coarse[...], anom[:, cols], preferred_element_type=f32)
            prod = mixed * modes[:, cols].astype(f32)
            sums = jnp.concatenate(
                [
                    jnp.sum(prod[:, j * BLK : (j + 1) * BLK], axis=0, keepdims=True)
                    for j in range(STEP)
                ],
                axis=0,
            )
            win[pl.ds(block, STEP), :] = sums.astype(bf16)
            return carry

        lax.fori_loop(0, half_blocks // 2 // STEP, body, 0)

    for q in range(2):
        for copy in loads[q]:
            copy.wait()
        increments(0, q)

    pl.semaphore_wait(barrier, greeted)

    idx_copies = []
    for d in range(1, slots):
        copy = remote(idxs.at[0], idxs.at[d], idx_sem, d, slot_plus(d))
        copy.start()
        idx_copies.append(copy)
    edge_copies = []
    for d in range(slots):
        copy = remote(
            win.at[pl.ds(half_at[0], HB)],
            edges.at[pl.ds(d * HB, HB)],
            edge_sem,
            d,
            slot_plus(d, outer),
        )
        copy.start()
        edge_copies.append(copy)

    for q in range(2):
        for copy in loads[2 + q]:
            copy.wait()
        increments(1, q)
    inner_copy = remote(
        win.at[pl.ds(half_at[1], HB)], win.at[pl.ds(blocks, HB)], core_sem, 0, partner
    )
    inner_copy.start()

    origin = s * reach
    outer_at = core * (HB + blocks)
    inner_at = HB + blocks - outer_at
    along = lax.broadcasted_iota(jnp.int32, (obs, BLK), 1)
    down = lax.broadcasted_iota(jnp.int32, (BLK, obs), 0)

    def hot(condition):
        return jnp.where(condition, 1.0, 0.0).astype(bf16)

    mine = jnp.broadcast_to(idxs[0, 0:1, :].astype(f32), (obs, BLK))
    mine_column = jnp.transpose(mine)
    for d in range(slots):
        at = lax.rem(s + slots - d, slots) * reach + outer_at
        edge_pick[:, d * HB : (d + 1) * HB] = hot(mine_column == (along + at).astype(f32))
        edge_add[d * HB : (d + 1) * HB, :] = hot(mine == (down + at).astype(f32))
    for d in range(slots):
        if d > 0:
            idx_copies[d - 1].wait_recv()
        listed = jnp.broadcast_to(idxs[d, 0:1, :].astype(f32), (obs, BLK))
        column = jnp.transpose(listed)
        for q in range(blocks // BLK + 1):
            at = origin + (HB + q * BLK if q < blocks // BLK else inner_at)
            pick_hot[d, :, q * BLK : (q + 1) * BLK] = hot(column == (along + at).astype(f32))
            add_hot[q * BLK : (q + 1) * BLK, d * obs : (d + 1) * obs] = hot(
                listed == (down + at).astype(f32)
            )

    inner_copy.wait_recv()
    pick_copies = []
    for d in range(1, slots):
        picks[d] = jnp.dot(pick_hot[d], win[...], preferred_element_type=f32).astype(bf16)
        copy = remote(picks.at[d], got.at[d], pick_sem, d, slot_minus(d))
        copy.start()
        pick_copies.append(copy)
    total = jnp.dot(pick_hot[0], win[...], preferred_element_type=f32)
    load_interp.wait()
    load_innov.wait()
    load_wt.wait()
    for copy in edge_copies:
        copy.wait_recv()
    total = total + jnp.dot(edge_pick[...], edges[...], preferred_element_type=f32)
    for d in range(1, slots):
        pick_copies[d - 1].wait_recv()
        total = total + got[d].astype(f32)
    states[...] = total.astype(bf16)

    live = cnt_ref[0, 0]
    sub = lax.broadcasted_iota(jnp.int32, (STEP, BLK), 0)

    def observe(g, carry):
        first = pl.multiple_of(g * STEP, STEP)
        mats = interp[pl.ds(first, STEP)].reshape(STEP * BLK, BLK)
        mapped_all = lax.dot_general(
            states[pl.ds(first, STEP), :], mats, NT, preferred_element_type=f32
        )
        mapped = mapped_all[:, 0:BLK]
        for r in range(1, STEP):
            mapped = jnp.where(sub == r, mapped_all[:, r * BLK : (r + 1) * BLK], mapped)
        misfit = jnp.where(
            sub + first < live, mapped - innov[pl.ds(first, STEP), :], jnp.zeros_like(mapped)
        )
        dep[pl.ds(first, STEP), :] = misfit
        weighted = wt[pl.ds(first, STEP), :] * misfit
        spread_w = jnp.concatenate(
            [jnp.where(sub == r, weighted, 0.0).astype(bf16) for r in range(STEP)], axis=1
        )
        pulled[pl.ds(first, STEP), :] = jnp.dot(
            spread_w, mats, preferred_element_type=f32
        ).astype(bf16)
        return carry

    lax.fori_loop(0, obs // STEP, observe, 0)

    pull_copies = []
    for d in range(1, slots):
        copy = remote(
            pulled.at[pl.ds(0, obs)], pulled.at[pl.ds(d * obs, obs)], pull_sem, d, slot_plus(d)
        )
        copy.start()
        pull_copies.append(copy)
    edge_out[...] = jnp.dot(
        edge_add[...], pulled[0:obs, :], preferred_element_type=f32
    ).astype(bf16)
    back_copies = []
    for d in range(slots):
        copy = remote(
            edge_out.at[pl.ds(d * HB, HB)],
            edge_back.at[d],
            back_sem,
            d,
            (lax.rem(s + slots - d, slots), outer),
        )
        copy.start()
        back_copies.append(copy)
    store_dep = pltpu.make_async_copy(dep, dep_hbm, local_sem.at[base + 3])
    store_dep.start()
    for copy in pull_copies:
        copy.wait_recv()

    inner_out[...] = jnp.dot(
        add_hot[blocks : blocks + HB, :], pulled[...], preferred_element_type=f32
    ).astype(bf16)
    inner_send = remote(inner_out, inner_back, core_sem, 1, partner)
    inner_send.start()
    adj[...] = jnp.dot(add_hot[0:blocks, :], pulled[...], preferred_element_type=f32)
    extra = None
    for d in range(slots):
        back_copies[d].wait_recv()
        got_edge = edge_back[d].astype(f32)
        extra = got_edge if extra is None else extra + got_edge
    outer_half = pl.ds(half_at[0], HB)
    adj[outer_half, :] = adj[outer_half, :] + extra

    def project(h):
        def body(i, acc):
            block = pl.multiple_of(half_at[h] + i * STEP, STEP)
            cols = pl.ds(pl.multiple_of(block * BLK, STEP * BLK), STEP * BLK)
            rows_adj = adj[pl.ds(block, STEP), :]
            part = modes[:, cols].astype(f32)
            scaled = jnp.concatenate(
                [
                    (part[:, j * BLK : (j + 1) * BLK] * rows_adj[j : j + 1, :]).astype(bf16)
                    for j in range(STEP)
                ],
                axis=1,
            )
            return acc + lax.dot_general(anom[:, cols], scaled, NT, preferred_element_type=f32)

        return body

    steps = half_blocks // STEP
    acc = lax.fori_loop(0, steps, project(0), jnp.zeros((members, width), f32))
    inner_send.wait_recv()
    inner_half = pl.ds(half_at[1], HB)
    adj[inner_half, :] = adj[inner_half, :] + inner_back[...].astype(f32)
    acc = lax.fori_loop(0, steps, project(1), acc)

    share_rows = members // tiles
    wide = jnp.concatenate([acc] * per_row, axis=1)
    wide = jnp.where(lane // width == lax.rem(member, share_rows), wide, 0.0)
    for j in range(tiles):
        gs[j % 2, j // 2] = jnp.sum(
            wide[j * share_rows : (j + 1) * share_rows, :], axis=0, keepdims=True
        )

    core_send = remote(gs.at[1 - core], gp, core_sem, 2, partner)
    core_send.start()
    core_send.wait_recv()
    gs[core] = gs[core] + gp[...]
    g_copies = []
    for d in range(slots):
        for e in range(chips):
            if d or e:
                to = lax.rem(z + e, chips)
                i = d * chips + e
                copy = remote(
                    gs.at[core, to],
                    gr.at[i],
                    g_sem,
                    i,
                    (lax.rem(s + d, slots), to * 2 + core),
                )
                copy.start()
                g_copies.append(copy)

    share = members * width // tiles
    per_line = BLK // share
    line = ctl_ref[pl.ds(t // per_line, 1), :]
    own = line
    for q in range(1, per_line):
        moved = jnp.concatenate([line[:, q * share :], line[:, : q * share]], axis=1)
        own = jnp.where(lax.rem(t, per_line) == q, moved, own)

    result = gs[core, z]
    for copy in g_copies:
        copy.wait_recv()
    for i in range(1, slots * chips):
        result = result + gr[i]
    grad_ref[...] = own + result

    store_dep.wait()
    for copy in (
        idx_copies
        + edge_copies
        + [inner_copy]
        + pick_copies
        + pull_copies
        + back_copies
        + [inner_send, core_send]
        + g_copies
    ):
        copy.wait_send()


def deliver(dep_in, grad_in, dep_out, grad_out, sem):
    pair = (
        pltpu.make_async_copy(dep_in, dep_out, sem.at[0]),
        pltpu.make_async_copy(grad_in, grad_out, sem.at[1]),
    )
    for copy in pair:
        copy.start()
    for copy in pair:
        copy.wait()


def on_device(
    slots, tiles, control, anomalies, modes, interp, block_index, counts, innovation, obs_weight
):
    members, rows = anomalies.shape[1:]
    width = modes.shape[0]
    obs = interp.shape[1]
    blocks = rows // BLK
    near = blocks + HB
    f32 = jnp.float32
    bf16 = jnp.bfloat16
    vmem = pl.BlockSpec(memory_space=pltpu.VMEM)
    hbm = pl.BlockSpec(memory_space=pl.ANY)

    def sems(n):
        return pltpu.SemaphoreType.DMA((2, n))

    departure, grad = pl.pallas_call(
        functools.partial(kernel, slots, tiles),
        out_shape=(
            jax.ShapeDtypeStruct((obs, BLK), f32),
            jax.ShapeDtypeStruct((1, BLK), f32),
        ),
        in_specs=[vmem, vmem, pl.BlockSpec(memory_space=pltpu.SMEM)] + [hbm] * 5,
        out_specs=(hbm, vmem),
        scratch_shapes=[
            pltpu.VMEM((members, rows), bf16),
            pltpu.VMEM((width, rows), bf16),
            pltpu.VMEM((obs, BLK, BLK), bf16),
            pltpu.VMEM((obs, BLK), f32),
            pltpu.VMEM((obs, BLK), f32),
            pltpu.VMEM((obs, BLK), f32),
            pltpu.VMEM((width, members), bf16),
            pltpu.VMEM((slots, 8, BLK), jnp.int32),
            pltpu.VMEM((slots, obs, near), bf16),
            pltpu.VMEM((near, slots * obs), bf16),
            pltpu.VMEM((obs, slots * HB), bf16),
            pltpu.VMEM((slots * HB, obs), bf16),
            pltpu.VMEM((near, BLK), bf16),
            pltpu.VMEM((slots * HB, BLK), bf16),
            pltpu.VMEM((slots, obs, BLK), bf16),
            pltpu.VMEM((slots, obs, BLK), bf16),
            pltpu.VMEM((obs, BLK), bf16),
            pltpu.VMEM((slots * obs, BLK), bf16),
            pltpu.VMEM((slots * HB, BLK), bf16),
            pltpu.VMEM((slots, HB, BLK), bf16),
            pltpu.VMEM((HB, BLK), bf16),
            pltpu.VMEM((HB, BLK), bf16),
            pltpu.VMEM((blocks, BLK), f32),
            pltpu.VMEM((2, tiles // 2, 1, BLK), f32),
            pltpu.VMEM((tiles // 2, 1, BLK), f32),
            pltpu.VMEM((slots * tiles // 2, 1, BLK), f32),
            pltpu.SemaphoreType.DMA((12,)),
            sems(slots),
            sems(slots),
            sems(3),
            sems(slots),
            sems(slots),
            sems(slots),
            sems(slots * tiles // 2),
        ],
        compiler_params=pltpu.CompilerParams(
            collective_id=0, has_side_effects=True, vmem_limit_bytes=56 * 1024 * 1024
        ),
    )(
        control.reshape(-1, BLK),
        block_index,
        counts,
        anomalies[0],
        modes,
        interp[0],
        innovation[0],
        obs_weight[0],
    )
    departure, grad = pl.pallas_call(
        deliver,
        out_shape=(
            jax.ShapeDtypeStruct((obs, BLK), f32),
            jax.ShapeDtypeStruct((1, BLK), f32),
        ),
        in_specs=[hbm] * 2,
        out_specs=(hbm, hbm),
        scratch_shapes=[pltpu.SemaphoreType.DMA((2,))],
    )(departure, grad)
    gradient = grad[0, : control.shape[0] // tiles]
    return departure[None], gradient


def solution(mesh):
    in_specs = (
        P(),
        P("slot", None, "tile"),
        P(None, "tile"),
        P("slot", "tile", None, None),
        P("slot", "tile"),
        P("slot", "tile"),
        P("slot", "tile", None),
        P("slot", "tile", None),
    )
    out_specs = (P("slot", "tile", None), P("tile"))
    return jax.shard_map(
        functools.partial(on_device, mesh.shape["slot"], mesh.shape["tile"]),
        mesh=mesh,
        in_specs=in_specs,
        out_specs=out_specs,
        check_vma=False,
    )
```

time: 41 us -> 37.5 us (0.915)
  local copies, waits for them, and re-layouts: 1.47 us -> 0 us
  other arithmetic: 1.28 us -> 0 us
  Pallas kernels: 36.7 us -> 36 us
    pallas_call x1, Pallas kernels: 36.7 us -> 32.9 us  [on_device(): pl.pallas_call(functools.partial(kernel, slots, tiles), out_shape=(jax.Sh...]
    pallas_call x0 -> x1, Pallas kernels: none -> 3.12 us  [on_device(): pl.pallas_call(deliver, out_shape=(jax.ShapeDtypeStruct((obs, BLK), f32),...]
    unnamed x1 -> x0, local copies, waits for them, and re-layouts: 1.47 us -> none
    add x1 -> x0, other arithmetic: 1.28 us -> none  [on_device(): lax.dynamic_slice_in_dim(control, start, share, 0) + grad[0, :share]]
where the time goes in v2:
time: 37.5 us; the launch traced here: 37.3 us
  Pallas kernels  36 us (96%)
  between operations  1.29 us (3%)
    pallas_call x1, Pallas kernels, on_device(): pl.pallas_call(functools.partial(kernel, slots, tiles), out_shape=(jax.Sh...  32.9 us
    pallas_call x1, Pallas kernels, on_device(): pl.pallas_call(deliver, out_shape=(jax.ShapeDtypeStruct((obs, BLK), f32),...  3.12 us

profile of v2, /device:TPU:0, one launch (start us, length us, event | category | flops | bytes accessed | tf_op | source)
XLA Modules:
  0.0 37.3 jit_solution(13068161052500335990)
XLA Ops:
  1.3 32.9 %shard_map.95 = (f32[128,128]{1,0:T(8,128)}, f32[1,128]{1,0:T(1,128)}) custom-call(f32[8,128]{1,0:T(8,128)} %bitcast.11, s32[1,128]{1,0:T(1,128)} %idx_ref.1, s32[1,1]{1,0:T(1,128)S(6)} %copy.10.cnt_ref, bf16[64,32768]{1,0:T(8,128)(2,1)} %bitcast.7, bf16[16,32768]{1,0:T(8,128)(2,1)} %modes_hbm.1, bf16[128,128,128]{2,1,0:T(8,128)(2,1)} %bitcast.8, ...), custom_call_target="tpu_custom_call" | custom-call | tf_op jit(solution)/shard_map/pallas_call | solution.py:432
  34.2 3.1 %shard_map.96 = (f32[128,128]{1,0:T(8,128)}, f32[1,128]{1,0:T(1,128)}) custom-call(f32[128,128]{1,0:T(8,128)} %get-tuple-element.6.dep_in, f32[1,128]{1,0:T(1,128)} %get-tuple-element.7.grad_in), custom_call_target="tpu_custom_call" | custom-call | tf_op jit(solution)/shard_map/pallas_call | solution.py:489

commit v3 on v2

--- a/solution.py
+++ b/solution.py
@@ -25,14 +25,13 @@
     interp_hbm,
     innov_hbm,
     wt_hbm,
-    dep_hbm,
+    dep_ref,
     grad_ref,
     anom,
     modes,
     interp,
     innov,
     wt,
-    dep,
     coarse,
     idxs,
     pick_hot,
@@ -94,6 +93,19 @@
             device_id_type=MESH,
         )
 
+    barrier = pltpu.get_barrier_semaphore()
+    pl.semaphore_signal(barrier, inc=1, device_id=partner, device_id_type=MESH)
+    greeted = 1
+    for d in range(slots):
+        for e in range(chips):
+            if d or e:
+                to = (lax.rem(s + d, slots), lax.rem(z + e, chips) * 2 + core)
+                pl.semaphore_signal(barrier, inc=1, device_id=to, device_id_type=MESH)
+                greeted += 1
+    for d in range(slots):
+        pl.semaphore_signal(barrier, inc=1, device_id=slot_plus(d, outer), device_id_type=MESH)
+        greeted += 1
+
     parts = 4
     part_rows = rows // parts
     starts = [
@@ -118,19 +130,6 @@
     load_interp.start()
     load_innov.start()
     load_wt.start()
-
-    barrier = pltpu.get_barrier_semaphore()
-    pl.semaphore_signal(barrier, inc=1, device_id=partner, device_id_type=MESH)
-    greeted = 1
-    for d in range(slots):
-        for e in range(chips):
-            if d or e:
-                to = (lax.rem(s + d, slots), lax.rem(z + e, chips) * 2 + core)
-                pl.semaphore_signal(barrier, inc=1, device_id=to, device_id_type=MESH)
-                greeted += 1
-    for d in range(slots):
-        pl.semaphore_signal(barrier, inc=1, device_id=slot_plus(d, outer), device_id_type=MESH)
-        greeted += 1
 
     idxs[0] = jnp.broadcast_to(idx_ref[...], (8, BLK))
 
@@ -173,7 +172,7 @@
             win[pl.ds(block, STEP), :] = sums.astype(bf16)
             return carry
 
-        lax.fori_loop(0, half_blocks // 2 // STEP, body, 0)
+        lax.fori_loop(0, half_blocks // 2 // STEP, body, 0, unroll=2)
 
     for q in range(2):
         for copy in loads[q]:
@@ -269,7 +268,7 @@
         misfit = jnp.where(
             sub + first < live, mapped - innov[pl.ds(first, STEP), :], jnp.zeros_like(mapped)
         )
-        dep[pl.ds(first, STEP), :] = misfit
+        dep_ref[pl.ds(first, STEP), :] = misfit
         weighted = wt[pl.ds(first, STEP), :] * misfit
         spread_w = jnp.concatenate(
             [jnp.where(sub == r, weighted, 0.0).astype(bf16) for r in range(STEP)], axis=1
@@ -279,7 +278,7 @@
         ).astype(bf16)
         return carry
 
-    lax.fori_loop(0, obs // STEP, observe, 0)
+    lax.fori_loop(0, obs // STEP, observe, 0, unroll=4)
 
     pull_copies = []
     for d in range(1, slots):
@@ -302,8 +301,6 @@
         )
         copy.start()
         back_copies.append(copy)
-    store_dep = pltpu.make_async_copy(dep, dep_hbm, local_sem.at[base + 3])
-    store_dep.start()
     for copy in pull_copies:
         copy.wait_recv()
 
@@ -339,11 +336,11 @@
         return body
 
     steps = half_blocks // STEP
-    acc = lax.fori_loop(0, steps, project(0), jnp.zeros((members, width), f32))
+    acc = lax.fori_loop(0, steps, project(0), jnp.zeros((members, width), f32), unroll=4)
     inner_send.wait_recv()
     inner_half = pl.ds(half_at[1], HB)
     adj[inner_half, :] = adj[inner_half, :] + inner_back[...].astype(f32)
-    acc = lax.fori_loop(0, steps, project(1), acc)
+    acc = lax.fori_loop(0, steps, project(1), acc, unroll=4)
 
     share_rows = members // tiles
     wide = jnp.concatenate([acc] * per_row, axis=1)
@@ -388,7 +385,6 @@
         result = result + gr[i]
     grad_ref[...] = own + result
 
-    store_dep.wait()
     for copy in (
         idx_copies
         + edge_copies
@@ -400,17 +396,6 @@
         + g_copies
     ):
         copy.wait_send()
-
-
-def deliver(dep_in, grad_in, dep_out, grad_out, sem):
-    pair = (
-        pltpu.make_async_copy(dep_in, dep_out, sem.at[0]),
-        pltpu.make_async_copy(grad_in, grad_out, sem.at[1]),
-    )
-    for copy in pair:
-        copy.start()
-    for copy in pair:
-        copy.wait()
 
 
 def on_device(
@@ -432,16 +417,15 @@
     departure, grad = pl.pallas_call(
         functools.partial(kernel, slots, tiles),
         out_shape=(
-            jax.ShapeDtypeStruct((obs, BLK), f32),
-            jax.ShapeDtypeStruct((1, BLK), f32),
+            pltpu.VMEM((obs, BLK), f32),
+            pltpu.VMEM((1, BLK), f32),
         ),
         in_specs=[vmem, vmem, pl.BlockSpec(memory_space=pltpu.SMEM)] + [hbm] * 5,
-        out_specs=(hbm, vmem),
+        out_specs=(vmem, vmem),
         scratch_shapes=[
             pltpu.VMEM((members, rows), bf16),
             pltpu.VMEM((width, rows), bf16),
             pltpu.VMEM((obs, BLK, BLK), bf16),
-            pltpu.VMEM((obs, BLK), f32),
             pltpu.VMEM((obs, BLK), f32),
             pltpu.VMEM((obs, BLK), f32),
             pltpu.VMEM((width, members), bf16),
@@ -464,7 +448,7 @@
             pltpu.VMEM((2, tiles // 2, 1, BLK), f32),
             pltpu.VMEM((tiles // 2, 1, BLK), f32),
             pltpu.VMEM((slots * tiles // 2, 1, BLK), f32),
-            pltpu.SemaphoreType.DMA((12,)),
+            pltpu.SemaphoreType.DMA((11,)),
             sems(slots),
             sems(slots),
             sems(3),
@@ -474,7 +458,7 @@
             sems(slots * tiles // 2),
         ],
         compiler_params=pltpu.CompilerParams(
-            collective_id=0, has_side_effects=True, vmem_limit_bytes=56 * 1024 * 1024
+            collective_id=0, has_side_effects=True, vmem_limit_bytes=61 * 1024 * 1024
         ),
     )(
         control.reshape(-1, BLK),
@@ -486,16 +470,6 @@
         innovation[0],
         obs_weight[0],
     )
-    departure, grad = pl.pallas_call(
-        deliver,
-        out_shape=(
-            jax.ShapeDtypeStruct((obs, BLK), f32),
-            jax.ShapeDtypeStruct((1, BLK), f32),
-        ),
-        in_specs=[hbm] * 2,
-        out_specs=(hbm, hbm),
-        scratch_shapes=[pltpu.SemaphoreType.DMA((2,))],
-    )(departure, grad)
     gradient = grad[0, : control.shape[0] // tiles]
     return departure[None], gradient
 

time: 37.5 us -> 32.6 us (0.87)
  Pallas kernels: 36 us -> 30 us
  local copies, waits for them, and re-layouts: 0 us -> 1.14 us
    pallas_call x2 -> x1, Pallas kernels: 36 us -> 30 us  [on_device(): pl.pallas_call(functools.partial(kernel, slots, tiles), out_shape=(pltpu....]
    unnamed x0 -> x2, local copies, waits for them, and re-layouts: none -> 1.14 us
where the time goes in v3:
time: 32.6 us; the launch traced here: 32.4 us
  Pallas kernels  30 us (92%)
  between operations  1.29 us (4%)
  local copies, waits for them, and re-layouts  1.14 us (3%)
    pallas_call x1, Pallas kernels, on_device(): pl.pallas_call(functools.partial(kernel, slots, tiles), out_shape=(pltpu....  30 us
    unnamed x2, local copies, waits for them, and re-layouts  1.14 us

profile of v3, /device:TPU:0, one launch (start us, length us, event | category | flops | bytes accessed | tf_op | source)
XLA Modules:
  0.0 32.4 jit_solution(18243940296535016579)
XLA Ops:
  1.3 30.0 %shard_map.95 = (f32[128,128]{1,0:T(8,128)S(1)}, f32[1,128]{1,0:T(1,128)S(1)}) custom-call(f32[8,128]{1,0:T(8,128)} %bitcast.13, s32[1,128]{1,0:T(1,128)} %idx_ref.1, s32[1,1]{1,0:T(1,128)S(6)} %copy.14.cnt_ref, bf16[64,32768]{1,0:T(8,128)(2,1)} %bitcast.9, bf16[16,32768]{1,0:T(8,128)(2,1)} %modes_hbm.1, bf16[128,128,128]{2,1,0:T(8,128)(2,1)} %bitcast.10, ...), custom_call_target="tpu_custom_call" | custom-call | tf_op jit(solution)/shard_map/pallas_call | solution.py:417
  31.2 0.6 %copy.12 = f32[1,128,128]{2,1,0:T(8,128)} copy(f32[1,128,128]{2,1,0:T(8,128)S(1)} %bitcast.7) | data formatting | bytes 131072
  31.9 0.5 %copy.13 = f32[128]{0:T(128)} copy(f32[128]{0:T(128)S(1)} %bitcast.8) | data formatting | bytes 1024

commit v4 on v3

--- a/solution.py
+++ b/solution.py
@@ -310,14 +310,6 @@
     inner_send = remote(inner_out, inner_back, core_sem, 1, partner)
     inner_send.start()
     adj[...] = jnp.dot(add_hot[0:blocks, :], pulled[...], preferred_element_type=f32)
-    extra = None
-    for d in range(slots):
-        back_copies[d].wait_recv()
-        got_edge = edge_back[d].astype(f32)
-        extra = got_edge if extra is None else extra + got_edge
-    outer_half = pl.ds(half_at[0], HB)
-    adj[outer_half, :] = adj[outer_half, :] + extra
-
     def project(h):
         def body(i, acc):
             block = pl.multiple_of(half_at[h] + i * STEP, STEP)
@@ -336,11 +328,18 @@
         return body
 
     steps = half_blocks // STEP
-    acc = lax.fori_loop(0, steps, project(0), jnp.zeros((members, width), f32), unroll=4)
     inner_send.wait_recv()
     inner_half = pl.ds(half_at[1], HB)
     adj[inner_half, :] = adj[inner_half, :] + inner_back[...].astype(f32)
-    acc = lax.fori_loop(0, steps, project(1), acc, unroll=4)
+    acc = lax.fori_loop(0, steps, project(1), jnp.zeros((members, width), f32), unroll=4)
+    extra = None
+    for d in range(slots):
+        back_copies[d].wait_recv()
+        got_edge = edge_back[d].astype(f32)
+        extra = got_edge if extra is None else extra + got_edge
+    outer_half = pl.ds(half_at[0], HB)
+    adj[outer_half, :] = adj[outer_half, :] + extra
+    acc = lax.fori_loop(0, steps, project(0), acc, unroll=4)
 
     share_rows = members // tiles
     wide = jnp.concatenate([acc] * per_row, axis=1)

time: 32.6 us -> 32.3 us (level)
  no operation moved by 1% of the time
where the time goes in v4:
time: 32.3 us; the launch traced here: 32.1 us
  Pallas kernels  29.7 us (92%)
  between operations  1.29 us (4%)
  local copies, waits for them, and re-layouts  1.14 us (4%)
    pallas_call x1, Pallas kernels, on_device(): pl.pallas_call(functools.partial(kernel, slots, tiles), out_shape=(pltpu....  29.7 us
    unnamed x2, local copies, waits for them, and re-layouts  1.14 us

profile of v4, /device:TPU:0, one launch (start us, length us, event | category | flops | bytes accessed | tf_op | source)
XLA Modules:
  0.0 32.1 jit_solution(2871855989451054992)
XLA Ops:
  1.3 29.7 %shard_map.95 = (f32[128,128]{1,0:T(8,128)S(1)}, f32[1,128]{1,0:T(1,128)S(1)}) custom-call(f32[8,128]{1,0:T(8,128)} %bitcast.13, s32[1,128]{1,0:T(1,128)} %idx_ref.1, s32[1,1]{1,0:T(1,128)S(6)} %copy.14.cnt_ref, bf16[64,32768]{1,0:T(8,128)(2,1)} %bitcast.9, bf16[16,32768]{1,0:T(8,128)(2,1)} %modes_hbm.1, bf16[128,128,128]{2,1,0:T(8,128)(2,1)} %bitcast.10, ...), custom_call_target="tpu_custom_call" | custom-call | tf_op jit(solution)/shard_map/pallas_call | solution.py:416
  31.0 0.6 %copy.12 = f32[1,128,128]{2,1,0:T(8,128)} copy(f32[1,128,128]{2,1,0:T(8,128)S(1)} %bitcast.7) | data formatting | bytes 131072
  31.6 0.5 %copy.13 = f32[128]{0:T(128)} copy(f32[128]{0:T(128)S(1)} %bitcast.8) | data formatting | bytes 1024
